TPU v7x, 512 devices: a whole 4x4x16 slice. The times are simulated.
512 devices in a mesh: row: 16 (over z), col: 4 (over y), depth: 8 (over x, core).
Axes of the slice: x: 4, y: 4, z: 16, core: 2. Of those that a mesh axis runs over, the one named last changes fastest.
Arguments:
- left_block: bfloat16 [6144, 6144], P('row', 'col'), may hold values from -6 to 6
- right_block: bfloat16 [6144, 12288], P('row', 'col'), may hold values from -0.078125 to 0.078125
Outputs:
- block_product: float32 [6144, 12288], P('row', ('col', 'depth'))
All inputs are finite; a program needn't handle non-finite values.
Results may differ from a plain program's by a relative error of at most 0.0003.
Values may be sent and summed in bfloat16 or wider, within the bound.
A program may use at most 64 MiB of HBM per device.

v0:
```python
import jax
import jax.numpy as jnp
from jax import lax
from jax.sharding import PartitionSpec as P


def on_device(left_block, right_block):
    layer_count = lax.axis_size("depth")
    layer = lax.axis_index("depth")
    out_cols = right_block.shape[1] // layer_count
    column_panel = lax.dynamic_slice_in_dim(right_block, layer * out_cols, out_cols, 1)
    full_left = lax.all_gather(left_block, "col", axis=1, tiled=True)
    full_panel = lax.all_gather(column_panel, "row", axis=0, tiled=True)
    return jnp.dot(full_left, full_panel, preferred_element_type=jnp.float32)


def solution(mesh):
    return jax.shard_map(
        on_device,
        mesh=mesh,
        in_specs=(P("row", "col"), P("row", "col")),
        out_specs=P("row", ("col", "depth")),
        check_vma=False,
    )
```

profile of v0, /device:TPU:24, one launch (start us, length us, event | category | flops | bytes accessed | tf_op | source)
XLA Modules:
  0.0 170.9 jit_solution(275525331861338446)
XLA Ops:
  6.5 0.0 copy-start
  6.5 0.0 all-gather.5.cloned.1.call-start
  6.5 0.7 all-gather.5.cloned.1.call-update
  7.3 0.0 all-gather.3.cloned.1.call-start
  7.3 0.9 copy-done
  8.2 0.7 constant_dynamic-slice_fusion
  8.9 0.0 all-gather.3.cloned.1.call-update
  9.0 63.2 %all-gather.5.cloned.1.call-done = bf16[384,6144]{1,0:T(8,128)(2,1)} async-done(((bf16[384,1536]{1,0:T(8,128)(2,1)}), bf16[384,6144]{1,0:T(8,128)(2,1)}) %all-gather.5.cloned.1.call-update) | async-done | bytes 4718608 | tf_op jit(solution)/shard_map/all_gather | solution.py:12
  72.2 84.4 %all-gather.3.cloned.1.call-done = bf16[6144,384]{1,0:T(8,128)(2,1)} async-done(((bf16[384,384]{1,0:T(8,128)(2,1)}), bf16[6144,384]{1,0:T(8,128)(2,1)}) %all-gather.3.cloned.1.call-update) | async-done | bytes 4718608 | tf_op jit(solution)/shard_map/all_gather | solution.py:13
  156.6 6.4 %convolution_bitcast_fusion = f32[384,384]{0,1:T(8,128)S(1)} fusion(bf16[6144,384]{1,0:T(8,128)(2,1)} %all-gather.3.cloned.1.call-done, bf16[384,6144]{1,0:T(8,128)(2,1)} %all-gather.5.cloned.1.call-done), kind=kOutput, calls=%fused_computation | convolution fusion | flops 1811939328 | bytes 10027008 | tf_op jit(solution)/shard_map/dot_general | solution.py:14
  163.1 1.1 copy.3
Async XLA Ops:
  6.5 1.7 copy-start
  6.5 65.7 %all-gather.5.cloned.1.call-start = ((), (), s32[]{:S(2)}) async-start(), calls=%async_computation.1 | async-start | bytes 5898240 | tf_op jit(solution)/shard_map/all_gather | solution.py:12
  7.3 149.4 %all-gather.3.cloned.1.call-start = ((), (), s32[]{:S(2)}) async-start(), calls=%async_computation | async-start | bytes 5013504 | tf_op jit(solution)/shard_map/all_gather | solution.py:13
Sparse Core Ops, SparseCore 0:
  9.5 62.7 all-gather.4
  74.3 82.3 all-gather.2
where the time goes:
time: 171 us
  waiting for transfers between devices  148 us (87%)
  between operations  13.4 us (8%)
  matrix products  6.4 us (4%)
  local copies, waits for them, and re-layouts  2.68 us (2%)
    all_gather x1, waiting for transfers between devices, on_device(): full_panel = lax.all_gather(column_panel, 'row', axis=0, tiled=True)  84.4 us
    all_gather x1, waiting for transfers between devices, on_device(): full_left = lax.all_gather(left_block, 'col', axis=1, tiled=True)  63.2 us
    dot_general x1, matrix products, on_device(): return jnp.dot(full_left, full_panel, preferred_element_type=jnp.float32)  6.4 us
  transfers between devices with their start and end apart: 2, of which 2 were waited for; matrix products, arithmetic and copies ran while one was open for 0% of the time, Pallas kernels for 0%

commit v1 on v0

v1 whole, which is shorter than its diff:
```python
import functools

import jax
import jax.numpy as jnp
from jax import lax
from jax.experimental import pallas as pl
from jax.experimental.pallas import tpu as pltpu
from jax.sharding import PartitionSpec as P

PIECES = 4
LEFT_NEAR = 3
LEFT_FAR = 4
LEFT_READY = 5


def kernel(
    left, right, out, lpan, rpan,
    own_sem, up_s, up_r, dn_s, dn_r, ly_s, ly_r, lc_s, lc_r,
):
    rows = lax.axis_size("row")
    cols = lax.axis_size("col")
    z, y, d = lax.axis_index("row"), lax.axis_index("col"), lax.axis_index("depth")
    depth, width = rpan.shape[1:]
    height = left.shape[0]
    half_steps = rows // 2
    piece = depth // PIECES
    per_col = left.shape[1] // depth

    z_up, z_dn = lax.rem(z + 1, rows), lax.rem(z + rows - 1, rows)
    y_up, y_dn = lax.rem(y + 1, cols), lax.rem(y + cols - 1, cols)
    y_far = lax.rem(y + 2, cols)
    core = lax.rem(d, 2)
    twin = d + 1 - 2 * core

    barrier = pltpu.get_barrier_semaphore()
    for who in ((z_up, y, d), (z_dn, y, d), (z, y_up, d), (z, y_dn, d), (z, y, twin)):
        pl.semaphore_signal(barrier, inc=1, device_id=who)
    pl.semaphore_wait(barrier, 5)

    my_cols = pl.ds(pl.multiple_of(d * width, 128), width)

    def up_rows(i):
        return pl.ds(i * piece, piece)

    def dn_rows(i):
        return pl.ds((i + PIECES // 2) % PIECES * piece, piece)

    def send(src, dst, send_sem, recv_sem, who):
        return pltpu.make_async_remote_copy(
            src_ref=src, dst_ref=dst, send_sem=send_sem, recv_sem=recv_sem,
            device_id=who,
        )

    def up_copy(step, i, first=False):
        chunk = lax.rem(z - step + 1 + rows, rows)
        dst = rpan.at[chunk, up_rows(i)]
        src = right.at[up_rows(i), my_cols] if first else dst
        return send(src, dst, up_s.at[step, i], up_r.at[step, i], (z_up, y, d))

    def dn_copy(step, i, first=False):
        chunk = lax.rem(z + step - 1, rows)
        dst = rpan.at[chunk, dn_rows(i)]
        src = right.at[dn_rows(i), my_cols] if first else dst
        return send(src, dst, dn_s.at[step, i], dn_r.at[step, i], (z_dn, y, d))

    def up_arrival(step, i):
        dst = rpan.at[lax.rem(z - step + rows, rows), up_rows(i)]
        return send(dst, dst, up_s.at[step, i], up_r.at[step, i], (z_up, y, d))

    def dn_arrival(step, i):
        dst = rpan.at[lax.rem(z + step, rows), dn_rows(i)]
        return send(dst, dst, dn_s.at[step, i], dn_r.at[step, i], (z_dn, y, d))

    for i in range(PIECES):
        up_copy(1, i, True).start()
        dn_copy(1, i, True).start()

    share = height // 2
    my_share = pl.ds(pl.multiple_of(core * share, 16), share)
    twin_share = pl.ds(pl.multiple_of((1 - core) * share, 16), share)
    first_part = pl.ds(pl.multiple_of(core * share, 16), share // 2)
    second_part = pl.ds(pl.multiple_of(core * share + share // 2, 16), share // 2)

    def near_copies():
        src, dst = left.at[my_share], lpan.at[y, my_share]
        return (
            send(src, dst, ly_s.at[0], ly_r.at[0], (z, y_up, d)),
            send(src, dst, ly_s.at[1], ly_r.at[1], (z, y_dn, d)),
        )

    def near_arrivals():
        a, b = lpan.at[y_dn, my_share], lpan.at[y_up, my_share]
        return (
            send(a, a, ly_s.at[0], ly_r.at[0], (z, y_up, d)),
            send(b, b, ly_s.at[1], ly_r.at[1], (z, y_dn, d)),
        )

    def far_copies():
        a, b = lpan.at[y_dn, first_part], lpan.at[y_up, second_part]
        return (
            send(a, a, ly_s.at[2], ly_r.at[2], (z, y_up, d)),
            send(b, b, ly_s.at[3], ly_r.at[3], (z, y_dn, d)),
        )

    def far_arrivals():
        a, b = lpan.at[y_far, first_part], lpan.at[y_far, second_part]
        return (
            send(a, a, ly_s.at[2], ly_r.at[2], (z, y_up, d)),
            send(b, b, ly_s.at[3], ly_r.at[3], (z, y_dn, d)),
        )

    def twin_copy(n, col, part):
        ref = lpan.at[col, part]
        return send(ref, ref, lc_s.at[n], lc_r.at[n], (z, y, twin))

    for c in near_copies():
        c.start()
    own_left = pltpu.make_async_copy(left, lpan.at[y], own_sem.at[0])
    own_right = pltpu.make_async_copy(right.at[:, my_cols], rpan.at[z], own_sem.at[1])
    own_left.start()
    own_right.start()
    out[...] = jnp.zeros_like(out)

    def add_product(chunk):
        col = chunk // per_col
        at = pl.ds(pl.multiple_of(lax.rem(chunk, per_col) * depth, 128), depth)
        out[...] += jnp.dot(
            lpan[col, :, at], rpan[chunk], preferred_element_type=jnp.float32
        )

    def entry_chunk(e):
        distance = (e + 1) // 2
        sign = 1 - 2 * lax.rem(e, 2)
        return lax.rem(z + sign * distance + rows, rows)

    per_step = -(-(rows - 1) // (half_steps - LEFT_READY))

    def ring_step(step, carry):
        for i in range(PIECES):
            up_arrival(step, i).wait_recv()
            if i < PIECES // 2:
                up_copy(step + 1, i).start()
            else:
                @pl.when(step < half_steps - 1)
                def _():
                    up_copy(step + 1, i).start()
            dn_arrival(step, i).wait_recv()
            if i < PIECES // 2:
                dn_copy(step + 1, i).start()
            else:
                @pl.when(step < half_steps - 1)
                def _():
                    dn_copy(step + 1, i).start()

        @pl.when(step == LEFT_NEAR)
        def _():
            for c in near_arrivals():
                c.wait_recv()
            for c in far_copies():
                c.start()
            twin_copy(0, y_dn, my_share).start()
            twin_copy(1, y_up, my_share).start()

        @pl.when(step == LEFT_FAR)
        def _():
            for c in far_arrivals():
                c.wait_recv()
            twin_copy(2, y_far, my_share).start()

        @pl.when(step == LEFT_READY)
        def _():
            own_left.wait()
            own_right.wait()
            for n, col in enumerate((y_dn, y_up, y_far)):
                twin_copy(n, col, twin_share).wait_recv()

        lo = jnp.maximum(step - LEFT_READY, 0) * per_step
        hi = jnp.minimum(jnp.maximum(step - LEFT_READY + 1, 0) * per_step, rows - 1)

        def body(e, c):
            add_product(entry_chunk(e))
            return c

        lax.fori_loop(lo, hi, body, 0)

        for i in range(PIECES):
            up_copy(step, i).wait_send()
            dn_copy(step, i).wait_send()
        return carry

    lax.fori_loop(1, half_steps, ring_step, 0)

    for c in near_copies() + far_copies():
        c.wait_send()
    for n, col in enumerate((y_dn, y_up, y_far)):
        twin_copy(n, col, my_share).wait_send()
    for i in range(PIECES // 2):
        up_arrival(half_steps, i).wait_recv()
        dn_arrival(half_steps, i).wait_recv()
    add_product(lax.rem(z + half_steps, rows))
    for i in range(PIECES // 2):
        up_copy(half_steps, i).wait_send()
        dn_copy(half_steps, i).wait_send()


def on_device(left_block, right_block):
    rows, cols = lax.axis_size("row"), lax.axis_size("col")
    layers = lax.axis_size("depth")
    height, left_cols = left_block.shape
    depth, right_cols = right_block.shape
    width = right_cols // layers
    steps = rows // 2 + 1
    dma = pltpu.SemaphoreType.DMA
    return pl.pallas_call(
        kernel,
        out_shape=jax.ShapeDtypeStruct((height, width), jnp.float32),
        in_specs=[pl.BlockSpec(memory_space=pl.ANY)] * 2,
        out_specs=pl.BlockSpec(memory_space=pltpu.VMEM),
        scratch_shapes=[
            pltpu.VMEM((cols, height, left_cols), jnp.bfloat16),
            pltpu.VMEM((rows, depth, width), jnp.bfloat16),
            dma((2,)),
            dma((steps, PIECES)),
            dma((steps, PIECES)),
            dma((steps, PIECES)),
            dma((steps, PIECES)),
            dma((4,)),
            dma((4,)),
            dma((3,)),
            dma((3,)),
        ],
        compiler_params=pltpu.CompilerParams(
            collective_id=0, has_side_effects=True, vmem_limit_bytes=48 << 20
        ),
        cost_estimate=pl.CostEstimate(
            flops=2 * height * width * depth * rows,
            bytes_accessed=2 * height * left_cols + 2 * depth * width + 4 * height * width,
            transcendentals=0,
        ),
    )(left_block, right_block)


def solution(mesh):
    return jax.shard_map(
        on_device,
        mesh=mesh,
        in_specs=(P("row", "col"), P("row", "col")),
        out_specs=P("row", ("col", "depth")),
        check_vma=False,
    )
```

time: 171 us -> 66.7 us (0.39)
  the two profiles are of different devices: /device:TPU:24 before, /device:TPU:2 now
where the time goes in v1:
time: 66.7 us; the launch traced here: 66.6 us
  Pallas kernels  62.8 us (94%)
  local copies, waits for them, and re-layouts  3.75 us (6%)
    pallas_call x1, Pallas kernels, on_device(): pl.pallas_call(kernel, out_shape=jax.ShapeDtypeStruct((height, width), jn...  62.8 us
    unnamed x5, local copies, waits for them, and re-layouts  3.75 us

profile of v1, /device:TPU:2, one launch (start us, length us, event | category | flops | bytes accessed | tf_op | source)
XLA Modules:
  0.0 66.6 jit_solution(6783650924342131184)
XLA Ops:
  0.0 0.0 copy-start
  0.0 1.7 %copy-done = bf16[384,3072]{1,0:T(8,128)(2,1)S(1)} copy-done((bf16[384,3072]{1,0:T(8,128)(2,1)S(1)}, bf16[384,3072]{1,0:T(8,128)(2,1)}, u32[]{:S(2)}) %copy-start) | copy-done | bytes 2359320
  1.7 0.0 copy-start.1
  1.7 1.3 %copy-done.1 = bf16[384,1536]{1,0:T(8,128)(2,1)S(1)} copy-done((bf16[384,1536]{1,0:T(8,128)(2,1)S(1)}, bf16[384,1536]{1,0:T(8,128)(2,1)}, u32[]{:S(2)}) %copy-start.1) | copy-done | bytes 1179672
  2.9 62.8 %shard_map.28 = f32[384,384]{1,0:T(8,128)S(1)} custom-call(bf16[384,1536]{1,0:T(8,128)(2,1)S(1)} %copy-done.1, bf16[384,3072]{1,0:T(8,128)(2,1)S(1)} %copy-done), custom_call_target="tpu_custom_call" | custom-call | flops 1811939328 | bytes 2064384 | tf_op jit(solution)/shard_map/pallas_call | solution.py:214
  65.8 0.8 %copy.4 = f32[384,384]{1,0:T(8,128)} copy(f32[384,384]{1,0:T(8,128)S(1)} %shard_map.28) | data formatting | bytes 1179648
Async XLA Ops:
  0.0 1.7 %copy-start = (bf16[384,3072]{1,0:T(8,128)(2,1)S(1)}, bf16[384,3072]{1,0:T(8,128)(2,1)}, u32[]{:S(2)}) copy-start(bf16[384,3072]{1,0:T(8,128)(2,1)} %right.1) | copy-start | bytes 7077892
  1.7 1.3 %copy-start.1 = (bf16[384,1536]{1,0:T(8,128)(2,1)S(1)}, bf16[384,1536]{1,0:T(8,128)(2,1)}, u32[]{:S(2)}) copy-start(bf16[384,1536]{1,0:T(8,128)(2,1)} %left.1) | copy-start | bytes 3538948

commit v2 on v1

--- a/solution.py
+++ b/solution.py
@@ -15,7 +15,7 @@
 
 def kernel(
     left, right, out, lpan, rpan,
-    own_sem, up_s, up_r, dn_s, dn_r, ly_s, ly_r, lc_s, lc_r,
+    answer, own_sem, up_s, up_r, dn_s, dn_r, ly_s, ly_r, lc_s, lc_r,
 ):
     rows = lax.axis_size("row")
     cols = lax.axis_size("col")
@@ -32,12 +32,46 @@
     core = lax.rem(d, 2)
     twin = d + 1 - 2 * core
 
+    my_cols = pl.ds(pl.multiple_of(d * width, 128), width)
+    own_right = pltpu.make_async_copy(right.at[:, my_cols], rpan.at[z], own_sem.at[1])
+    own_left = pltpu.make_async_copy(left, lpan.at[y], own_sem.at[0])
+    own_right.start()
+    own_left.start()
+
+    turned = jnp.logical_and(z == 0, d == 0)
+    up, dn, right_of, left_of, beside = range(5)
+    peers = ((z_up, y, d), (z_dn, y, d), (z, y_up, d), (z, y_dn, d), (z, y, twin))
+    greets = (
+        z != rows - 1,
+        z == 0,
+        jnp.logical_xor(y != cols - 1, turned),
+        jnp.logical_xor(y == 0, turned),
+        core == 1,
+    )
+    back = (dn, up, left_of, right_of, beside)
+
     barrier = pltpu.get_barrier_semaphore()
-    for who in ((z_up, y, d), (z_dn, y, d), (z, y_up, d), (z, y_dn, d), (z, y, twin)):
-        pl.semaphore_signal(barrier, inc=1, device_id=who)
-    pl.semaphore_wait(barrier, 5)
-
-    my_cols = pl.ds(pl.multiple_of(d * width, 128), width)
+    greeted = 0
+    for who, first in zip(peers, greets):
+        greeted = greeted + jnp.where(first, 0, 1)
+
+        @pl.when(first)
+        def _():
+            pl.semaphore_signal(barrier, inc=1, device_id=who)
+
+    @pl.when(greeted > 0)
+    def _():
+        pl.semaphore_wait(barrier, greeted)
+
+    for side, (who, first) in enumerate(zip(peers, greets)):
+        @pl.when(jnp.logical_not(first))
+        def _():
+            pl.semaphore_signal(answer.at[back[side]], inc=1, device_id=who)
+
+    def admitted(side):
+        @pl.when(greets[side])
+        def _():
+            pl.semaphore_wait(answer.at[side], 1)
 
     def up_rows(i):
         return pl.ds(i * piece, piece)
@@ -51,17 +85,15 @@
             device_id=who,
         )
 
-    def up_copy(step, i, first=False):
+    def up_copy(step, i):
         chunk = lax.rem(z - step + 1 + rows, rows)
         dst = rpan.at[chunk, up_rows(i)]
-        src = right.at[up_rows(i), my_cols] if first else dst
-        return send(src, dst, up_s.at[step, i], up_r.at[step, i], (z_up, y, d))
-
-    def dn_copy(step, i, first=False):
+        return send(dst, dst, up_s.at[step, i], up_r.at[step, i], (z_up, y, d))
+
+    def dn_copy(step, i):
         chunk = lax.rem(z + step - 1, rows)
         dst = rpan.at[chunk, dn_rows(i)]
-        src = right.at[dn_rows(i), my_cols] if first else dst
-        return send(src, dst, dn_s.at[step, i], dn_r.at[step, i], (z_dn, y, d))
+        return send(dst, dst, dn_s.at[step, i], dn_r.at[step, i], (z_dn, y, d))
 
     def up_arrival(step, i):
         dst = rpan.at[lax.rem(z - step + rows, rows), up_rows(i)]
@@ -71,9 +103,20 @@
         dst = rpan.at[lax.rem(z + step, rows), dn_rows(i)]
         return send(dst, dst, dn_s.at[step, i], dn_r.at[step, i], (z_dn, y, d))
 
+    def start_dn():
+        admitted(dn)
+        for i in range(PIECES):
+            dn_copy(1, i).start()
+
+    own_right.wait()
+
+    @pl.when(z != 0)
+    def _():
+        start_dn()
+
+    admitted(up)
     for i in range(PIECES):
-        up_copy(1, i, True).start()
-        dn_copy(1, i, True).start()
+        up_copy(1, i).start()
 
     share = height // 2
     my_share = pl.ds(pl.multiple_of(core * share, 16), share)
@@ -82,7 +125,7 @@
     second_part = pl.ds(pl.multiple_of(core * share + share // 2, 16), share // 2)
 
     def near_copies():
-        src, dst = left.at[my_share], lpan.at[y, my_share]
+        src = dst = lpan.at[y, my_share]
         return (
             send(src, dst, ly_s.at[0], ly_r.at[0], (z, y_up, d)),
             send(src, dst, ly_s.at[1], ly_r.at[1], (z, y_dn, d)),
@@ -113,13 +156,16 @@
         ref = lpan.at[col, part]
         return send(ref, ref, lc_s.at[n], lc_r.at[n], (z, y, twin))
 
+    own_left.wait()
+    admitted(right_of)
+    admitted(left_of)
     for c in near_copies():
         c.start()
-    own_left = pltpu.make_async_copy(left, lpan.at[y], own_sem.at[0])
-    own_right = pltpu.make_async_copy(right.at[:, my_cols], rpan.at[z], own_sem.at[1])
-    own_left.start()
-    own_right.start()
     out[...] = jnp.zeros_like(out)
+
+    @pl.when(z == 0)
+    def _():
+        start_dn()
 
     def add_product(chunk):
         col = chunk // per_col
@@ -135,22 +181,26 @@
 
     per_step = -(-(rows - 1) // (half_steps - LEFT_READY))
 
+    def last_up(at, i):
+        return at != 0 if i < PIECES // 2 else False
+
+    def last_dn(at, i):
+        return True if i < PIECES // 2 else at == 0
+
     def ring_step(step, carry):
         for i in range(PIECES):
             up_arrival(step, i).wait_recv()
-            if i < PIECES // 2:
+
+            @pl.when(jnp.logical_or(step < half_steps - 1, last_up(z_up, i)))
+            def _():
                 up_copy(step + 1, i).start()
-            else:
-                @pl.when(step < half_steps - 1)
-                def _():
-                    up_copy(step + 1, i).start()
+
             dn_arrival(step, i).wait_recv()
-            if i < PIECES // 2:
+
+            @pl.when(jnp.logical_or(step < half_steps - 1, last_dn(z_dn, i)))
+            def _():
                 dn_copy(step + 1, i).start()
-            else:
-                @pl.when(step < half_steps - 1)
-                def _():
-                    dn_copy(step + 1, i).start()
+
 
         @pl.when(step == LEFT_NEAR)
         def _():
@@ -158,6 +208,7 @@
                 c.wait_recv()
             for c in far_copies():
                 c.start()
+            admitted(beside)
             twin_copy(0, y_dn, my_share).start()
             twin_copy(1, y_up, my_share).start()
 
@@ -169,8 +220,6 @@
 
         @pl.when(step == LEFT_READY)
         def _():
-            own_left.wait()
-            own_right.wait()
             for n, col in enumerate((y_dn, y_up, y_far)):
                 twin_copy(n, col, twin_share).wait_recv()
 
@@ -194,13 +243,24 @@
         c.wait_send()
     for n, col in enumerate((y_dn, y_up, y_far)):
         twin_copy(n, col, my_share).wait_send()
-    for i in range(PIECES // 2):
-        up_arrival(half_steps, i).wait_recv()
-        dn_arrival(half_steps, i).wait_recv()
+    for i in range(PIECES):
+        @pl.when(last_up(z, i))
+        def _():
+            up_arrival(half_steps, i).wait_recv()
+
+        @pl.when(last_dn(z, i))
+        def _():
+            dn_arrival(half_steps, i).wait_recv()
+
     add_product(lax.rem(z + half_steps, rows))
-    for i in range(PIECES // 2):
-        up_copy(half_steps, i).wait_send()
-        dn_copy(half_steps, i).wait_send()
+    for i in range(PIECES):
+        @pl.when(last_up(z_up, i))
+        def _():
+            up_copy(half_steps, i).wait_send()
+
+        @pl.when(last_dn(z_dn, i))
+        def _():
+            dn_copy(half_steps, i).wait_send()
 
 
 def on_device(left_block, right_block):
@@ -213,12 +273,13 @@
     dma = pltpu.SemaphoreType.DMA
     return pl.pallas_call(
         kernel,
-        out_shape=jax.ShapeDtypeStruct((height, width), jnp.float32),
+        out_shape=pltpu.VMEM((height, width), jnp.float32),
         in_specs=[pl.BlockSpec(memory_space=pl.ANY)] * 2,
         out_specs=pl.BlockSpec(memory_space=pltpu.VMEM),
         scratch_shapes=[
             pltpu.VMEM((cols, height, left_cols), jnp.bfloat16),
             pltpu.VMEM((rows, depth, width), jnp.bfloat16),
+            pltpu.SemaphoreType.REGULAR((5,)),
             dma((2,)),
             dma((steps, PIECES)),
             dma((steps, PIECES)),
@@ -230,7 +291,7 @@
             dma((3,)),
         ],
         compiler_params=pltpu.CompilerParams(
-            collective_id=0, has_side_effects=True, vmem_limit_bytes=48 << 20
+            collective_id=0, has_side_effects=True, vmem_limit_bytes=63 << 20
         ),
         cost_estimate=pl.CostEstimate(
             flops=2 * height * width * depth * rows,

time: 66.7 us -> 61.1 us (0.916)
  the two profiles are of different devices: /device:TPU:2 before, /device:TPU:24 now
where the time goes in v2:
time: 61.1 us; the launch traced here: 60.7 us
  Pallas kernels  59.8 us (98%)
  local copies, waits for them, and re-layouts  0.82 us (1%)
    pallas_call x1, Pallas kernels, on_device(): pl.pallas_call(kernel, out_shape=pltpu.VMEM((height, width), jnp.float32)...  59.8 us

profile of v2, /device:TPU:24, one launch (start us, length us, event | category | flops | bytes accessed | tf_op | source)
XLA Modules:
  0.0 60.7 jit_solution(9243061556476761083)
XLA Ops:
  0.0 59.8 %shard_map.28 = f32[384,384]{1,0:T(8,128)S(1)} custom-call(bf16[384,1536]{1,0:T(8,128)(2,1)} %left.1, bf16[384,3072]{1,0:T(8,128)(2,1)} %right.1), custom_call_target="tpu_custom_call" | custom-call | flops 1811939328 | bytes 2064384 | tf_op jit(solution)/shard_map/pallas_call | solution.py:274
  59.8 0.8 %copy.4 = f32[384,384]{1,0:T(8,128)} copy(f32[384,384]{1,0:T(8,128)S(1)} %shard_map.28) | data formatting | bytes 1179648

commit v3 on v2

--- a/solution.py
+++ b/solution.py
@@ -8,6 +8,8 @@
 from jax.sharding import PartitionSpec as P
 
 PIECES = 4
+FROM_BELOW = {0: 28, 1: 29, 15: 32}
+LAG = {0: 4, 1: 2, 2: 1}
 LEFT_NEAR = 3
 LEFT_FAR = 4
 LEFT_READY = 5
@@ -73,11 +75,8 @@
         def _():
             pl.semaphore_wait(answer.at[side], 1)
 
-    def up_rows(i):
-        return pl.ds(i * piece, piece)
-
-    def dn_rows(i):
-        return pl.ds((i + PIECES // 2) % PIECES * piece, piece)
+    def part(i):
+        return pl.ds(pl.multiple_of(i * piece, 16), piece)
 
     def send(src, dst, send_sem, recv_sem, who):
         return pltpu.make_async_remote_copy(
@@ -85,28 +84,30 @@
             device_id=who,
         )
 
-    def up_copy(step, i):
-        chunk = lax.rem(z - step + 1 + rows, rows)
-        dst = rpan.at[chunk, up_rows(i)]
-        return send(dst, dst, up_s.at[step, i], up_r.at[step, i], (z_up, y, d))
-
-    def dn_copy(step, i):
-        chunk = lax.rem(z + step - 1, rows)
-        dst = rpan.at[chunk, dn_rows(i)]
-        return send(dst, dst, dn_s.at[step, i], dn_r.at[step, i], (z_dn, y, d))
-
-    def up_arrival(step, i):
-        dst = rpan.at[lax.rem(z - step + rows, rows), up_rows(i)]
-        return send(dst, dst, up_s.at[step, i], up_r.at[step, i], (z_up, y, d))
-
-    def dn_arrival(step, i):
-        dst = rpan.at[lax.rem(z + step, rows), dn_rows(i)]
-        return send(dst, dst, dn_s.at[step, i], dn_r.at[step, i], (z_dn, y, d))
+    def up_copy(at):
+        chunk = lax.rem(z - at // PIECES + rows, rows)
+        ref = rpan.at[chunk, part(lax.rem(at, PIECES))]
+        return send(ref, ref, up_s.at[at], up_r.at[at], (z_up, y, d))
+
+    def dn_copy(at):
+        chunk = lax.rem(z + at // PIECES, rows)
+        ref = rpan.at[chunk, part(PIECES - 1 - lax.rem(at, PIECES))]
+        return send(ref, ref, dn_s.at[at], dn_r.at[at], (z_dn, y, d))
+
+    def up_arrival(at):
+        chunk = lax.rem(z - at // PIECES - 1 + rows, rows)
+        ref = rpan.at[chunk, part(lax.rem(at, PIECES))]
+        return send(ref, ref, up_s.at[at], up_r.at[at], (z_up, y, d))
+
+    def dn_arrival(at):
+        chunk = lax.rem(z + at // PIECES + 1, rows)
+        ref = rpan.at[chunk, part(PIECES - 1 - lax.rem(at, PIECES))]
+        return send(ref, ref, dn_s.at[at], dn_r.at[at], (z_dn, y, d))
 
     def start_dn():
         admitted(dn)
         for i in range(PIECES):
-            dn_copy(1, i).start()
+            dn_copy(i).start()
 
     own_right.wait()
 
@@ -116,7 +117,7 @@
 
     admitted(up)
     for i in range(PIECES):
-        up_copy(1, i).start()
+        up_copy(i).start()
 
     share = height // 2
     my_share = pl.ds(pl.multiple_of(core * share, 16), share)
@@ -176,31 +177,62 @@
 
     def entry_chunk(e):
         distance = (e + 1) // 2
-        sign = 1 - 2 * lax.rem(e, 2)
+        sign = 2 * lax.rem(e, 2) - 1
         return lax.rem(z + sign * distance + rows, rows)
 
-    per_step = -(-(rows - 1) // (half_steps - LEFT_READY))
-
-    def last_up(at, i):
-        return at != 0 if i < PIECES // 2 else False
-
-    def last_dn(at, i):
-        return True if i < PIECES // 2 else at == 0
-
-    def ring_step(step, carry):
+    total = (rows - 1) * PIECES
+
+    def below(at):
+        count = total // 2
+        for plane, pieces in FROM_BELOW.items():
+            count = jnp.where(at == plane, pieces, count)
+        return count
+
+    mine_up, mine_dn = below(z), total - below(z)
+    next_up, next_dn = below(z_up), total - below(z_dn)
+    lag = 0
+    for plane, pieces in LAG.items():
+        lag = jnp.where(z == plane, pieces, lag)
+
+    def ring_step(step):
         for i in range(PIECES):
-            up_arrival(step, i).wait_recv()
-
-            @pl.when(jnp.logical_or(step < half_steps - 1, last_up(z_up, i)))
+            at_dn = (step - 1) * PIECES + i
+            at_up = at_dn - lag
+
+            @pl.when(jnp.logical_and(at_up >= 0, at_up < mine_up))
             def _():
-                up_copy(step + 1, i).start()
-
-            dn_arrival(step, i).wait_recv()
-
-            @pl.when(jnp.logical_or(step < half_steps - 1, last_dn(z_dn, i)))
+                up_arrival(at_up).wait_recv()
+
+                @pl.when(at_up + PIECES < next_up)
+                def _():
+                    up_copy(at_up + PIECES).start()
+
+            @pl.when(at_dn < mine_dn)
             def _():
-                dn_copy(step + 1, i).start()
-
+                dn_arrival(at_dn).wait_recv()
+
+                @pl.when(at_dn + PIECES < next_dn)
+                def _():
+                    dn_copy(at_dn + PIECES).start()
+
+    def sent(step):
+        for i in range(PIECES):
+            at = (step - 1) * PIECES + i
+
+            @pl.when(at < next_up)
+            def _():
+                up_copy(at).wait_send()
+
+            @pl.when(at < next_dn)
+            def _():
+                dn_copy(at).wait_send()
+
+    near = half_steps - 2
+    entries = 2 * near
+    per_step = -(-entries // (near - LEFT_READY + 1))
+
+    def near_step(step, carry):
+        ring_step(step)
 
         @pl.when(step == LEFT_NEAR)
         def _():
@@ -224,7 +256,7 @@
                 twin_copy(n, col, twin_share).wait_recv()
 
         lo = jnp.maximum(step - LEFT_READY, 0) * per_step
-        hi = jnp.minimum(jnp.maximum(step - LEFT_READY + 1, 0) * per_step, rows - 1)
+        hi = jnp.minimum(jnp.maximum(step - LEFT_READY + 1, 0) * per_step, entries)
 
         def body(e, c):
             add_product(entry_chunk(e))
@@ -232,35 +264,37 @@
 
         lax.fori_loop(lo, hi, body, 0)
 
-        for i in range(PIECES):
-            up_copy(step, i).wait_send()
-            dn_copy(step, i).wait_send()
+        @pl.when(step > 1)
+        def _():
+            sent(step - 1)
+
         return carry
 
-    lax.fori_loop(1, half_steps, ring_step, 0)
-
-    for c in near_copies() + far_copies():
-        c.wait_send()
-    for n, col in enumerate((y_dn, y_up, y_far)):
-        twin_copy(n, col, my_share).wait_send()
-    for i in range(PIECES):
-        @pl.when(last_up(z, i))
-        def _():
-            up_arrival(half_steps, i).wait_recv()
-
-        @pl.when(last_dn(z, i))
-        def _():
-            dn_arrival(half_steps, i).wait_recv()
-
-    add_product(lax.rem(z + half_steps, rows))
-    for i in range(PIECES):
-        @pl.when(last_up(z_up, i))
-        def _():
-            up_copy(half_steps, i).wait_send()
-
-        @pl.when(last_dn(z_dn, i))
-        def _():
-            dn_copy(half_steps, i).wait_send()
+    lax.fori_loop(1, near + 1, near_step, 0)
+
+    def far_step(step, carry):
+        ring_step(step)
+        sent(step - 1)
+
+        @pl.when(step == near + 1)
+        def _():
+            for c in near_copies() + far_copies():
+                c.wait_send()
+            for n, col in enumerate((y_dn, y_up, y_far)):
+                twin_copy(n, col, my_share).wait_send()
+
+        def body(e, c):
+            add_product(entry_chunk(e))
+            return c
+
+        count = jnp.where(lag == 0, 3, 2)
+        lo = jnp.where(step == near + 1, 0, jnp.where(step == near + 3, count, 3))
+        hi = jnp.where(step == near + 1, count, jnp.where(step == near + 3, 4, 3))
+        lax.fori_loop(entries + lo, entries + hi, body, 0)
+        return carry
+
+    lax.fori_loop(near + 1, near + 4, far_step, 0)
+    sent(near + 3)
 
 
 def on_device(left_block, right_block):
@@ -269,7 +303,7 @@
     height, left_cols = left_block.shape
     depth, right_cols = right_block.shape
     width = right_cols // layers
-    steps = rows // 2 + 1
+    order = (rows // 2 + 1) * PIECES
     dma = pltpu.SemaphoreType.DMA
     return pl.pallas_call(
         kernel,
@@ -281,10 +315,10 @@
             pltpu.VMEM((rows, depth, width), jnp.bfloat16),
             pltpu.SemaphoreType.REGULAR((5,)),
             dma((2,)),
-            dma((steps, PIECES)),
-            dma((steps, PIECES)),
-            dma((steps, PIECES)),
-            dma((steps, PIECES)),
+            dma((order,)),
+            dma((order,)),
+            dma((order,)),
+            dma((order,)),
             dma((4,)),
             dma((4,)),
             dma((3,)),

time: 61.1 us -> 59.4 us (0.972)
  Pallas kernels: 59.8 us -> 58.5 us
    pallas_call x1, Pallas kernels: 59.8 us -> 58.5 us  [on_device(): pl.pallas_call(kernel, out_shape=pltpu.VMEM((height, width), jnp.float32)...]
where the time goes in v3:
time: 59.4 us; the launch traced here: 59.3 us
  Pallas kernels  58.5 us (98%)
  local copies, waits for them, and re-layouts  0.82 us (1%)
    pallas_call x1, Pallas kernels, on_device(): pl.pallas_call(kernel, out_shape=pltpu.VMEM((height, width), jnp.float32)...  58.5 us

profile of v3, /device:TPU:24, one launch (start us, length us, event | category | flops | bytes accessed | tf_op | source)
XLA Modules:
  0.0 59.3 jit_solution(11118167411450487937)
XLA Ops:
  0.0 58.5 %shard_map.28 = f32[384,384]{1,0:T(8,128)S(1)} custom-call(bf16[384,1536]{1,0:T(8,128)(2,1)} %left.1, bf16[384,3072]{1,0:T(8,128)(2,1)} %right.1), custom_call_target="tpu_custom_call" | custom-call | flops 1811939328 | bytes 2064384 | tf_op jit(solution)/shard_map/pallas_call | solution.py:308
  58.5 0.8 %copy.4 = f32[384,384]{1,0:T(8,128)} copy(f32[384,384]{1,0:T(8,128)S(1)} %shard_map.28) | data formatting | bytes 1179648

commit v4 on v3

v4 whole, which is shorter than its diff:
```python
import functools

import jax
import jax.numpy as jnp
from jax import lax
from jax.experimental import pallas as pl
from jax.experimental.pallas import tpu as pltpu
from jax.sharding import PartitionSpec as P

PIECES = 4
TAKES = 3 * PIECES + 1
FROM_BELOW = {0: (27, 28), 1: (28, 28), 15: (32, 32)}
LAG = {0: 4, 1: 3, 2: 2, 3: 1}
LEFT_NEAR = 3
LEFT_FAR = 4
LEFT_READY = 5
PER_TURN = 2


def kernel(
    left, right, out, lpan, rpan,
    answer, own_sem, up_s, up_r, dn_s, dn_r, left_s, left_r,
):
    rows = lax.axis_size("row")
    cols = lax.axis_size("col")
    z, y, d = lax.axis_index("row"), lax.axis_index("col"), lax.axis_index("depth")
    depth, width = right.shape[0], rpan.shape[1]
    height = left.shape[0]
    half_steps = rows // 2
    piece = depth // PIECES
    per_col = left.shape[1] // depth

    z_up, z_dn = lax.rem(z + 1, rows), lax.rem(z + rows - 1, rows)
    y_up, y_dn = lax.rem(y + 1, cols), lax.rem(y + cols - 1, cols)
    y_far = lax.rem(y + 2, cols)
    core = lax.rem(d, 2)
    twin = d + 1 - 2 * core

    def chunk_rows(chunk, first=0, size=depth):
        return rpan.at[pl.ds(pl.multiple_of(chunk * depth + first, 16), size)]

    def left_rows(col, first=0, size=height):
        return lpan.at[pl.ds(pl.multiple_of(col * height + first, 16), size)]

    my_cols = pl.ds(pl.multiple_of(d * width, 128), width)
    own_right = pltpu.make_async_copy(right.at[:, my_cols], chunk_rows(z), own_sem.at[1])
    own_left = pltpu.make_async_copy(left, left_rows(y), own_sem.at[0])
    own_right.start()
    own_left.start()

    turned = jnp.logical_and(z == 0, d == 0)
    up, dn, right_of, left_of, beside = range(5)
    peers = ((z_up, y, d), (z_dn, y, d), (z, y_up, d), (z, y_dn, d), (z, y, twin))
    greets = (
        z < rows - 2,
        jnp.logical_or(z == 0, z == rows - 1),
        jnp.logical_xor(y != cols - 1, turned),
        jnp.logical_xor(y == 0, turned),
        core == 1,
    )
    back = (dn, up, left_of, right_of, beside)

    barrier = pltpu.get_barrier_semaphore()
    greeted = 0
    for who, first in zip(peers, greets):
        greeted = greeted + jnp.where(first, 0, 1)

        @pl.when(first)
        def _():
            pl.semaphore_signal(barrier, inc=1, device_id=who)

    @pl.when(greeted > 0)
    def _():
        pl.semaphore_wait(barrier, greeted)

    for side, (who, first) in enumerate(zip(peers, greets)):
        @pl.when(jnp.logical_not(first))
        def _():
            pl.semaphore_signal(answer.at[back[side]], inc=1, device_id=who)

    def admitted(side):
        @pl.when(greets[side])
        def _():
            pl.semaphore_wait(answer.at[side], 1)

    def part(chunk, i):
        return chunk_rows(chunk, i * piece, piece)

    def send(src, dst, send_sem, recv_sem, who):
        return pltpu.make_async_remote_copy(
            src_ref=src, dst_ref=dst, send_sem=send_sem, recv_sem=recv_sem,
            device_id=who,
        )

    def up_copy(at):
        chunk = lax.rem(z - at // PIECES + rows, rows)
        ref = part(chunk, lax.rem(at, PIECES))
        src = right.at[pl.ds(at * piece, piece), my_cols] if isinstance(at, int) else ref
        return send(src, ref, up_s.at[0], up_r.at[at % TAKES], (z_up, y, d))

    def dn_copy(at):
        chunk = lax.rem(z + at // PIECES, rows)
        ref = part(chunk, PIECES - 1 - lax.rem(at, PIECES))
        src = right.at[pl.ds((PIECES - 1 - at) * piece, piece), my_cols] if isinstance(at, int) else ref
        return send(src, ref, dn_s.at[0], dn_r.at[at % TAKES], (z_dn, y, d))

    def up_arrival(at):
        chunk = lax.rem(z - at // PIECES - 1 + rows, rows)
        ref = part(chunk, lax.rem(at, PIECES))
        return send(ref, ref, up_s.at[0], up_r.at[at % TAKES], (z_up, y, d))

    def dn_arrival(at):
        chunk = lax.rem(z + at // PIECES + 1, rows)
        ref = part(chunk, PIECES - 1 - lax.rem(at, PIECES))
        return send(ref, ref, dn_s.at[0], dn_r.at[at % TAKES], (z_dn, y, d))

    def start_dn():
        admitted(dn)
        for i in range(PIECES):
            dn_copy(i).start()

    outer = jnp.logical_or(z == 0, z == rows - 1)

    @pl.when(jnp.logical_not(outer))
    def _():
        start_dn()

    admitted(up)
    for i in range(PIECES):
        up_copy(i).start()

    @pl.when(z == rows - 1)
    def _():
        start_dn()

    share = height // 2
    mine = core * share
    to_right, to_left, to_twin = (z, y_up, d), (z, y_dn, d), (z, y, twin)

    def near_copies():
        ref = left_rows(y, mine, share)
        return (
            send(ref, ref, left_s.at[0], left_r.at[0], to_right),
            send(ref, ref, left_s.at[0], left_r.at[0], to_left),
        )

    def far_copies():
        a = left_rows(y_dn, mine, share // 2)
        b = left_rows(y_up, mine + share // 2, share // 2)
        return (
            send(a, a, left_s.at[0], left_r.at[1], to_right),
            send(b, b, left_s.at[0], left_r.at[1], to_left),
        )

    def twin_copy(col):
        ref = left_rows(col, mine, share)
        return send(ref, ref, left_s.at[1], left_r.at[2], to_twin)

    def all_of(size, which_s, which_r):
        ref = lpan.at[pl.ds(0, size)]
        return send(ref, ref, left_s.at[which_s], left_r.at[which_r], to_twin)

    own_left.wait()
    own_right.wait()
    admitted(right_of)
    admitted(left_of)
    for c in near_copies():
        c.start()
    out[...] = jnp.zeros_like(out)

    @pl.when(z == 0)
    def _():
        start_dn()

    def add_product(chunk):
        col = chunk // per_col
        at = pl.ds(pl.multiple_of(lax.rem(chunk, per_col) * depth, 128), depth)
        out[...] += jnp.dot(
            left_rows(col)[:, at], chunk_rows(chunk)[...], preferred_element_type=jnp.float32
        )

    total = (rows - 1) * PIECES

    def below(at):
        count = total // 2
        for plane, pieces in FROM_BELOW.items():
            count = jnp.where(at == plane, jnp.where(core == 0, *pieces), count)
        return count

    mine_up, mine_dn = below(z), total - below(z)
    next_up, next_dn = below(z_up), total - below(z_dn)
    lag = 0
    for plane, pieces in LAG.items():
        lag = jnp.where(z == plane, pieces, lag)

    def all_sent(count, sem, counts):
        for n in sorted(counts):
            ref = rpan.at[pl.ds(0, n * piece)]

            @pl.when(count == n)
            def _():
                send(ref, ref, sem.at[0], up_r.at[0], (z_up, y, d)).wait_send()

    seven = half_steps - 1
    whole_7 = jnp.where(mine_up >= seven * PIECES, seven * PIECES - 1 + lag, mine_dn - 1)
    whole_8 = jnp.where(
        mine_dn >= half_steps * PIECES,
        half_steps * PIECES - 1,
        jnp.maximum(mine_up - 1 + lag, mine_dn - 1),
    )
    turn_round = whole_8 < whole_7
    whole_first = jnp.minimum(whole_7, whole_8)
    whole_second = jnp.maximum(whole_7, whole_8)
    regular = 2 * seven

    def entry_chunk(e):
        e = jnp.where(jnp.logical_and(turn_round, e >= regular), 2 * regular + 1 - e, e)
        distance = (e + 1) // 2
        sign = 2 * lax.rem(e, 2) - 1
        return lax.rem(z + sign * distance + rows, rows)

    def whole_after(at):
        from_above = jnp.minimum((at + 1) // PIECES, seven)
        from_below = jnp.clip((at + 1 - lag) // PIECES, 0, seven - 1)
        count = 2 * from_below + jnp.where(from_above > from_below, 2, 1)
        more = jnp.where(at >= whole_first, 1, 0) + jnp.where(at >= whole_second, 1, 0)
        return count + jnp.where(count == regular, more, 0)

    turns = jnp.maximum(mine_up + lag, mine_dn)

    def take(at, done):
        at_up = at - lag

        @pl.when(jnp.logical_and(at_up >= 0, at_up < mine_up))
        def _():
            up_arrival(at_up).wait_recv()

            @pl.when(at_up + PIECES < next_up)
            def _():
                up_copy(at_up + PIECES).start()

        @pl.when(at < mine_dn)
        def _():
            dn_arrival(at).wait_recv()

            @pl.when(at + PIECES < next_dn)
            def _():
                dn_copy(at + PIECES).start()

        @pl.when(at == LEFT_NEAR * PIECES)
        def _():
            all_of(2 * share, 0, 0).wait_recv()
            for c in far_copies():
                c.start()
            admitted(beside)
            twin_copy(y_dn).start()
            twin_copy(y_up).start()

        @pl.when(at == LEFT_FAR * PIECES)
        def _():
            all_of(share, 0, 1).wait_recv()
            twin_copy(y_far).start()

        @pl.when(at == LEFT_READY * PIECES)
        def _():
            all_of(3 * share, 1, 2).wait_recv()
            all_of(3 * share, 0, 0).wait_send()
            all_of(3 * share, 1, 0).wait_send()

        whole = jnp.where(at < LEFT_READY * PIECES, 0, whole_after(at))
        upto = jnp.where(at == turns - 1, whole, jnp.minimum(whole, done + PER_TURN))

        def body(e, c):
            add_product(entry_chunk(e))
            return c

        lax.fori_loop(done, upto, body, 0)
        return upto

    lax.fori_loop(0, turns, take, 0)
    counts = {total // 2}.union(*FROM_BELOW.values())
    all_sent(next_up, up_s, counts)
    all_sent(next_dn, dn_s, {total - n for n in counts})


def on_device(left_block, right_block):
    rows, cols = lax.axis_size("row"), lax.axis_size("col")
    layers = lax.axis_size("depth")
    height, left_cols = left_block.shape
    depth, right_cols = right_block.shape
    width = right_cols // layers
    dma = pltpu.SemaphoreType.DMA
    return pl.pallas_call(
        kernel,
        out_shape=pltpu.VMEM((height, width), jnp.float32),
        in_specs=[pl.BlockSpec(memory_space=pl.ANY)] * 2,
        out_specs=pl.BlockSpec(memory_space=pltpu.VMEM),
        scratch_shapes=[
            pltpu.VMEM((cols * height, left_cols), jnp.bfloat16),
            pltpu.VMEM((rows * depth, width), jnp.bfloat16),
            pltpu.SemaphoreType.REGULAR((5,)),
            dma((2,)),
            dma((1,)),
            dma((TAKES,)),
            dma((1,)),
            dma((TAKES,)),
            dma((2,)),
            dma((3,)),
        ],
        compiler_params=pltpu.CompilerParams(
            collective_id=0, has_side_effects=True, vmem_limit_bytes=63 << 20
        ),
        cost_estimate=pl.CostEstimate(
            flops=2 * height * width * depth * rows,
            bytes_accessed=2 * height * left_cols + 2 * depth * width + 4 * height * width,
            transcendentals=0,
        ),
    )(left_block, right_block)


def solution(mesh):
    return jax.shard_map(
        on_device,
        mesh=mesh,
        in_specs=(P("row", "col"), P("row", "col")),
        out_specs=P("row", ("col", "depth")),
        check_vma=False,
    )
```

time: 59.4 us -> 57.1 us (0.961)
  Pallas kernels: 58.5 us -> 56.2 us
    pallas_call x1, Pallas kernels: 58.5 us -> 56.2 us  [on_device(): pl.pallas_call(kernel, out_shape=pltpu.VMEM((height, width), jnp.float32)...]
where the time goes in v4:
time: 57.1 us; the launch traced here: 57 us
  Pallas kernels  56.2 us (98%)
  local copies, waits for them, and re-layouts  0.82 us (1%)
    pallas_call x1, Pallas kernels, on_device(): pl.pallas_call(kernel, out_shape=pltpu.VMEM((height, width), jnp.float32)...  56.2 us

profile of v4, /device:TPU:24, one launch (start us, length us, event | category | flops | bytes accessed | tf_op | source)
XLA Modules:
  0.0 57.0 jit_solution(12058702932095667760)
XLA Ops:
  0.0 56.2 %shard_map.28 = f32[384,384]{1,0:T(8,128)S(1)} custom-call(bf16[384,1536]{1,0:T(8,128)(2,1)} %left.1, bf16[384,3072]{1,0:T(8,128)(2,1)} %right.1), custom_call_target="tpu_custom_call" | custom-call | flops 1811939328 | bytes 2064384 | tf_op jit(solution)/shard_map/pallas_call | solution.py:293
  56.2 0.8 %copy.4 = f32[384,384]{1,0:T(8,128)} copy(f32[384,384]{1,0:T(8,128)S(1)} %shard_map.28) | data formatting | bytes 1179648

commit v5 on v4

--- a/solution.py
+++ b/solution.py
@@ -15,6 +15,7 @@
 LEFT_FAR = 4
 LEFT_READY = 5
 PER_TURN = 2
+BLOCK = 128
 
 
 def kernel(
@@ -202,28 +203,53 @@
                 send(ref, ref, sem.at[0], up_r.at[0], (z_up, y, d)).wait_send()
 
     seven = half_steps - 1
-    whole_7 = jnp.where(mine_up >= seven * PIECES, seven * PIECES - 1 + lag, mine_dn - 1)
-    whole_8 = jnp.where(
-        mine_dn >= half_steps * PIECES,
-        half_steps * PIECES - 1,
-        jnp.maximum(mine_up - 1 + lag, mine_dn - 1),
-    )
-    turn_round = whole_8 < whole_7
-    whole_first = jnp.minimum(whole_7, whole_8)
-    whole_second = jnp.maximum(whole_7, whole_8)
     regular = 2 * seven
+    blocks = depth // BLOCK
+    swapped = mine_up < seven * PIECES
+
+    def piece_at(distance, i):
+        at = (distance - 1) * PIECES + i
+        other = (rows - distance - 1) * PIECES + PIECES - 1 - i
+        return jnp.where(at < mine_up, at + lag, other)
+
+    def block_at(distance, n):
+        first, last = n * BLOCK // piece, ((n + 1) * BLOCK - 1) // piece
+        return functools.reduce(
+            jnp.maximum, [piece_at(distance, i) for i in range(first, last + 1)]
+        )
+
+    ready = []
+    for n in range(blocks):
+        low, high = block_at(seven, n), block_at(half_steps, blocks - 1 - n)
+        if n == blocks - 1:
+            low, high = jnp.where(swapped, high, low), jnp.where(swapped, low, high)
+        ready += [low, high]
+    for n in range(1, len(ready)):
+        ready[n] = jnp.maximum(ready[n], ready[n - 1])
 
     def entry_chunk(e):
-        e = jnp.where(jnp.logical_and(turn_round, e >= regular), 2 * regular + 1 - e, e)
         distance = (e + 1) // 2
         sign = 2 * lax.rem(e, 2) - 1
         return lax.rem(z + sign * distance + rows, rows)
+
+    def add_block(e):
+        e = jnp.where(jnp.logical_and(swapped, e >= 2 * blocks - 2), 4 * blocks - 3 - e, e)
+        upper = lax.rem(e, 2)
+        chunk = lax.rem(z + half_steps + 1 - upper, rows)
+        n = jnp.where(upper == 1, blocks - 1 - e // 2, e // 2)
+        col = chunk // per_col
+        at = lax.rem(chunk, per_col) * depth + n * BLOCK
+        out[...] += jnp.dot(
+            left_rows(col)[:, pl.ds(pl.multiple_of(at, 128), BLOCK)],
+            chunk_rows(chunk, n * BLOCK, BLOCK)[...],
+            preferred_element_type=jnp.float32,
+        )
 
     def whole_after(at):
         from_above = jnp.minimum((at + 1) // PIECES, seven)
         from_below = jnp.clip((at + 1 - lag) // PIECES, 0, seven - 1)
         count = 2 * from_below + jnp.where(from_above > from_below, 2, 1)
-        more = jnp.where(at >= whole_first, 1, 0) + jnp.where(at >= whole_second, 1, 0)
+        more = sum(jnp.where(at >= r, 1, 0) for r in ready)
         return count + jnp.where(count == regular, more, 0)
 
     turns = jnp.maximum(mine_up + lag, mine_dn)
@@ -271,7 +297,14 @@
         upto = jnp.where(at == turns - 1, whole, jnp.minimum(whole, done + PER_TURN))
 
         def body(e, c):
-            add_product(entry_chunk(e))
+            @pl.when(e < regular)
+            def _():
+                add_product(entry_chunk(e))
+
+            @pl.when(e >= regular)
+            def _():
+                add_block(e - regular)
+
             return c
 
         lax.fori_loop(done, upto, body, 0)

time: 57.1 us -> 57.5 us (level)
  no operation moved by 1% of the time
where the time goes in v5:
time: 57.5 us; the launch traced here: 57.4 us
  Pallas kernels  56.6 us (98%)
  local copies, waits for them, and re-layouts  0.82 us (1%)
    pallas_call x1, Pallas kernels, on_device(): pl.pallas_call(kernel, out_shape=pltpu.VMEM((height, width), jnp.float32)...  56.6 us

profile of v5, /device:TPU:24, one launch (start us, length us, event | category | flops | bytes accessed | tf_op | source)
XLA Modules:
  0.0 57.4 jit_solution(1819495410282392872)
XLA Ops:
  0.0 56.6 %shard_map.28 = f32[384,384]{1,0:T(8,128)S(1)} custom-call(bf16[384,1536]{1,0:T(8,128)(2,1)} %left.1, bf16[384,3072]{1,0:T(8,128)(2,1)} %right.1), custom_call_target="tpu_custom_call" | custom-call | flops 1811939328 | bytes 2064384 | tf_op jit(solution)/shard_map/pallas_call | solution.py:326
  56.6 0.8 %copy.4 = f32[384,384]{1,0:T(8,128)} copy(f32[384,384]{1,0:T(8,128)S(1)} %shard_map.28) | data formatting | bytes 1179648

commit v6 on v4

--- a/solution.py
+++ b/solution.py
@@ -45,8 +45,6 @@
     my_cols = pl.ds(pl.multiple_of(d * width, 128), width)
     own_right = pltpu.make_async_copy(right.at[:, my_cols], chunk_rows(z), own_sem.at[1])
     own_left = pltpu.make_async_copy(left, left_rows(y), own_sem.at[0])
-    own_right.start()
-    own_left.start()
 
     turned = jnp.logical_and(z == 0, d == 0)
     up, dn, right_of, left_of, beside = range(5)
@@ -133,15 +131,19 @@
     def _():
         start_dn()
 
+    own_left.start()
+    own_right.start()
+
     share = height // 2
     mine = core * share
     to_right, to_left, to_twin = (z, y_up, d), (z, y_dn, d), (z, y, twin)
 
     def near_copies():
         ref = left_rows(y, mine, share)
+        src = left.at[pl.ds(pl.multiple_of(mine, 16), share)]
         return (
-            send(ref, ref, left_s.at[0], left_r.at[0], to_right),
-            send(ref, ref, left_s.at[0], left_r.at[0], to_left),
+            send(src, ref, left_s.at[0], left_r.at[0], to_right),
+            send(src, ref, left_s.at[0], left_r.at[0], to_left),
         )
 
     def far_copies():
@@ -160,8 +162,6 @@
         ref = lpan.at[pl.ds(0, size)]
         return send(ref, ref, left_s.at[which_s], left_r.at[which_r], to_twin)
 
-    own_left.wait()
-    own_right.wait()
     admitted(right_of)
     admitted(left_of)
     for c in near_copies():
@@ -228,8 +228,15 @@
 
     turns = jnp.maximum(mine_up + lag, mine_dn)
 
+    counts = {total // 2}.union(*FROM_BELOW.values())
+
     def take(at, done):
         at_up = at - lag
+
+        @pl.when(at == turns - 1)
+        def _():
+            all_sent(next_up, up_s, counts)
+            all_sent(next_dn, dn_s, {total - n for n in counts})
 
         @pl.when(jnp.logical_and(at_up >= 0, at_up < mine_up))
         def _():
@@ -263,6 +270,8 @@
 
         @pl.when(at == LEFT_READY * PIECES)
         def _():
+            own_left.wait()
+            own_right.wait()
             all_of(3 * share, 1, 2).wait_recv()
             all_of(3 * share, 0, 0).wait_send()
             all_of(3 * share, 1, 0).wait_send()
@@ -278,9 +287,6 @@
         return upto
 
     lax.fori_loop(0, turns, take, 0)
-    counts = {total // 2}.union(*FROM_BELOW.values())
-    all_sent(next_up, up_s, counts)
-    all_sent(next_dn, dn_s, {total - n for n in counts})
 
 
 def on_device(left_block, right_block):

time: 57.1 us -> 57.1 us (level)
  no operation moved by 1% of the time
where the time goes in v6:
time: 57.1 us; the launch traced here: 57 us
  Pallas kernels  56.2 us (98%)
  local copies, waits for them, and re-layouts  0.82 us (1%)
    pallas_call x1, Pallas kernels, on_device(): pl.pallas_call(kernel, out_shape=pltpu.VMEM((height, width), jnp.float32)...  56.2 us

profile of v6, /device:TPU:24, one launch (start us, length us, event | category | flops | bytes accessed | tf_op | source)
XLA Modules:
  0.0 57.0 jit_solution(2214639146754306361)
XLA Ops:
  0.0 56.2 %shard_map.28 = f32[384,384]{1,0:T(8,128)S(1)} custom-call(bf16[384,1536]{1,0:T(8,128)(2,1)} %left.1, bf16[384,3072]{1,0:T(8,128)(2,1)} %right.1), custom_call_target="tpu_custom_call" | custom-call | flops 1811939328 | bytes 2064384 | tf_op jit(solution)/shard_map/pallas_call | solution.py:299
  56.2 0.8 %copy.4 = f32[384,384]{1,0:T(8,128)} copy(f32[384,384]{1,0:T(8,128)S(1)} %shard_map.28) | data formatting | bytes 1179648

commit v7 on v6

--- a/solution.py
+++ b/solution.py
@@ -9,8 +9,8 @@
 
 PIECES = 4
 TAKES = 3 * PIECES + 1
-FROM_BELOW = {0: (27, 28), 1: (28, 28), 15: (32, 32)}
-LAG = {0: 4, 1: 3, 2: 2, 3: 1}
+FROM_BELOW = {0: (27, 28), 1: (28, 29), 15: (32, 32)}
+LAG = {0: (4, 4), 1: (3, 2), 2: (2, 1), 3: (1, 1)}
 LEFT_NEAR = 3
 LEFT_FAR = 4
 LEFT_READY = 5
@@ -191,7 +191,7 @@
     next_up, next_dn = below(z_up), total - below(z_dn)
     lag = 0
     for plane, pieces in LAG.items():
-        lag = jnp.where(z == plane, pieces, lag)
+        lag = jnp.where(z == plane, jnp.where(core == 0, *pieces), lag)
 
     def all_sent(count, sem, counts):
         for n in sorted(counts):
@@ -228,15 +228,8 @@
 
     turns = jnp.maximum(mine_up + lag, mine_dn)
 
-    counts = {total // 2}.union(*FROM_BELOW.values())
-
     def take(at, done):
         at_up = at - lag
-
-        @pl.when(at == turns - 1)
-        def _():
-            all_sent(next_up, up_s, counts)
-            all_sent(next_dn, dn_s, {total - n for n in counts})
 
         @pl.when(jnp.logical_and(at_up >= 0, at_up < mine_up))
         def _():
@@ -287,6 +280,9 @@
         return upto
 
     lax.fori_loop(0, turns, take, 0)
+    counts = {total // 2}.union(*FROM_BELOW.values())
+    all_sent(next_up, up_s, counts)
+    all_sent(next_dn, dn_s, {total - n for n in counts})
 
 
 def on_device(left_block, right_block):

time: 57.1 us -> 57.1 us (level)
  no operation moved by 1% of the time
where the time goes in v7:
time: 57.1 us; the launch traced here: 57 us
  Pallas kernels  56.2 us (98%)
  local copies, waits for them, and re-layouts  0.82 us (1%)
    pallas_call x1, Pallas kernels, on_device(): pl.pallas_call(kernel, out_shape=pltpu.VMEM((height, width), jnp.float32)...  56.2 us

profile of v7, /device:TPU:24, one launch (start us, length us, event | category | flops | bytes accessed | tf_op | source)
XLA Modules:
  0.0 57.0 jit_solution(7254694953610150460)
XLA Ops:
  0.0 56.2 %shard_map.28 = f32[384,384]{1,0:T(8,128)S(1)} custom-call(bf16[384,1536]{1,0:T(8,128)(2,1)} %left.1, bf16[384,3072]{1,0:T(8,128)(2,1)} %right.1), custom_call_target="tpu_custom_call" | custom-call | flops 1811939328 | bytes 2064384 | tf_op jit(solution)/shard_map/pallas_call | solution.py:295
  56.2 0.8 %copy.4 = f32[384,384]{1,0:T(8,128)} copy(f32[384,384]{1,0:T(8,128)S(1)} %shard_map.28) | data formatting | bytes 1179648

commit v8 on v4

--- a/solution.py
+++ b/solution.py
@@ -11,9 +11,9 @@
 TAKES = 3 * PIECES + 1
 FROM_BELOW = {0: (27, 28), 1: (28, 28), 15: (32, 32)}
 LAG = {0: 4, 1: 3, 2: 2, 3: 1}
-LEFT_NEAR = 3
-LEFT_FAR = 4
-LEFT_READY = 5
+LEFT_NEAR = 2
+LEFT_FAR = 3
+LEFT_READY = 4
 PER_TURN = 2
 
 

time: 57.1 us -> 57.1 us (level)
  no operation moved by 1% of the time
where the time goes in v8:
time: 57.1 us; the launch traced here: 57 us
  Pallas kernels  56.2 us (98%)
  local copies, waits for them, and re-layouts  0.82 us (1%)
    pallas_call x1, Pallas kernels, on_device(): pl.pallas_call(kernel, out_shape=pltpu.VMEM((height, width), jnp.float32)...  56.2 us

profile of v8, /device:TPU:24, one launch (start us, length us, event | category | flops | bytes accessed | tf_op | source)
XLA Modules:
  0.0 57.0 jit_solution(1551122284827618188)
XLA Ops:
  0.0 56.2 %shard_map.28 = f32[384,384]{1,0:T(8,128)S(1)} custom-call(bf16[384,1536]{1,0:T(8,128)(2,1)} %left.1, bf16[384,3072]{1,0:T(8,128)(2,1)} %right.1), custom_call_target="tpu_custom_call" | custom-call | flops 1811939328 | bytes 2064384 | tf_op jit(solution)/shard_map/pallas_call | solution.py:293
  56.2 0.8 %copy.4 = f32[384,384]{1,0:T(8,128)} copy(f32[384,384]{1,0:T(8,128)S(1)} %shard_map.28) | data formatting | bytes 1179648
